TPU v7x, 32 devices: a whole 2x2x4 slice. The times are simulated.
32 devices in a mesh: grp: 2 (over x), tp: 16 (over z, y, core).
Axes of the slice: x: 2, y: 2, z: 4, core: 2. Of those that a mesh axis runs over, the one named last changes fastest.
Arguments:
- hidden_in: bfloat16 [768, 8192], P('grp', 'tp'), parts along dimension 0, may hold values from -30 to 30
- norm_gain: bfloat16 [8192], P('tp'), may hold values from 0.5 to 8
- w_query: bfloat16 [8192, 8192], P('tp'), may hold values from -0.0625 to 0.0625
- b_query: bfloat16 [8192], P('tp'), may hold values from -3 to 3
- key_weight_matrix: bfloat16 [8192, 1024], P('tp'), may hold values from -0.0625 to 0.0625
- key_offset_bias: bfloat16 [1024], replicated, may hold values from -3 to 3
- value_weight_matrix: bfloat16 [8192, 1024], P('tp'), may hold values from -0.0625 to 0.0625
- value_offset_bias: bfloat16 [1024], replicated, may hold values from -3 to 3
- w_out: bfloat16 [8192, 8192], P('tp'), may hold values from -0.25 to 0.25
- lengths: int32 [4], P('grp'), parts along dimension 0, may hold values from 24 to 192, as said below
Outputs:
- layer_out: bfloat16 [768, 8192], P('grp', 'tp'), parts along dimension 0
- rotated_key_cache: bfloat16 [768, 1024], P('grp', 'tp'), parts along dimension 0
- value_cache: bfloat16 [768, 1024], P('grp', 'tp'), parts along dimension 0
There are 2 independent parts, one for each index of `grp`. A program takes and returns all parts, laid end to end along the dimension named above; an argument that names none is the same for every part. Nothing has to cross between parts.
Inputs may be any that keep to these rules, and one draw needn't show every extreme that they name: `lengths`: at least one rollout fills all 192 slots; valid tokens lie at the start of a rollout's slots.
All inputs are finite; a program needn't handle non-finite values.
Results may differ from a plain program's by a relative error of at most 0.0055.
The roundings to bfloat16 on the way count: a program that leaves them out, or rounds other values in their place, can miss the bound.
Values may be sent and summed in bfloat16 or wider, within the bound.
A program may use at most 128 MiB of HBM per device.

v0:
```python
import jax
import jax.numpy as jnp
from jax import lax
from jax.sharding import PartitionSpec as P

QUERY_HEADS = 64
KEY_VALUE_HEADS = 8
HEAD_WIDTH = 128
ROLLOUT_SLOTS = 192
GROUP_ROLLOUTS = 2


NORM_EPS = 1e-06
ROPE_BASE = 1000000.0


def rotary_tables(values, cosine_table, sine_table):
    half_dim = values.shape[-1] // 2
    first_half = values[..., :half_dim]
    second_half = values[..., half_dim:]
    turned = jnp.concatenate([-second_half, first_half], axis=-1)
    return values * cosine_table[:, None, :] + turned * sine_table[:, None, :]


def local(
    hidden_in,
    norm_gain,
    w_query,
    b_query,
    key_weight_matrix,
    key_offset_bias,
    value_weight_matrix,
    value_offset_bias,
    w_out,
    lengths,
):
    tensor_parallel_count = lax.axis_size("tp")
    device_place = lax.axis_index("tp")
    query_group_width = tensor_parallel_count // KEY_VALUE_HEADS
    heads_dev = QUERY_HEADS // tensor_parallel_count
    token_count = hidden_in.shape[0]
    gathered, gain_all = (
        lax.all_gather(hidden_in, "tp", axis=1, tiled=True),
        lax.all_gather(norm_gain, "tp", axis=0, tiled=True),
    )
    full_x = gathered.astype(jnp.float32)
    mean_square = jnp.mean(full_x * full_x, axis=-1, keepdims=True)
    normed = (full_x * lax.rsqrt(mean_square + NORM_EPS) * gain_all.astype(jnp.float32)).astype(
        jnp.bfloat16
    )
    local_row_count = key_weight_matrix.shape[0]
    kv_head = device_place // query_group_width
    tile_width = HEAD_WIDTH // query_group_width
    offset = device_place % query_group_width * tile_width
    positions = jnp.arange(ROLLOUT_SLOTS, dtype=jnp.int32)
    valid_grid = positions[None, :] < lengths[:, None]
    valid_token_mask = valid_grid.reshape(-1)
    zero_half_precision = jnp.zeros((), jnp.bfloat16)
    key_repeated = jnp.repeat(
        key_weight_matrix.reshape(local_row_count, KEY_VALUE_HEADS, HEAD_WIDTH),
        query_group_width,
        axis=1,
    ).reshape(local_row_count, tensor_parallel_count * HEAD_WIDTH)
    value_repeated = jnp.repeat(
        value_weight_matrix.reshape(local_row_count, KEY_VALUE_HEADS, HEAD_WIDTH),
        query_group_width,
        axis=1,
    ).reshape(local_row_count, tensor_parallel_count * HEAD_WIDTH)
    query_cols, key_cols, value_cols = (
        lax.all_to_all(w_query, "tp", split_axis=1, concat_axis=0, tiled=True),
        lax.all_to_all(key_repeated, "tp", split_axis=1, concat_axis=0, tiled=True),
        lax.all_to_all(value_repeated, "tp", split_axis=1, concat_axis=0, tiled=True),
    )
    key_bias = lax.dynamic_slice_in_dim(key_offset_bias, kv_head * HEAD_WIDTH, HEAD_WIDTH)
    value_bias = lax.dynamic_slice_in_dim(value_offset_bias, kv_head * HEAD_WIDTH, HEAD_WIDTH)
    key_projected_rows = jnp.dot(
        normed, key_cols, preferred_element_type=jnp.float32
    ) + key_bias.astype(jnp.float32)
    value_rounded_rows = (
        jnp.dot(normed, value_cols, preferred_element_type=jnp.float32)
        + value_bias.astype(jnp.float32)
    ).astype(jnp.bfloat16)
    value_cache = lax.dynamic_slice_in_dim(
        jnp.where(valid_token_mask[:, None], value_rounded_rows, zero_half_precision),
        offset,
        tile_width,
        1,
    )
    queries = jnp.dot(normed, query_cols, preferred_element_type=jnp.float32) + b_query.astype(
        jnp.float32
    )
    pos_float = jnp.tile(positions, GROUP_ROLLOUTS).astype(jnp.float32)
    inverse_freq = jnp.power(
        ROPE_BASE, -2.0 * jnp.arange(HEAD_WIDTH // 2).astype(jnp.float32) / HEAD_WIDTH
    )
    angles = pos_float[:, None] * inverse_freq[None, :]
    cosine_table = jnp.concatenate([jnp.cos(angles), jnp.cos(angles)], axis=-1)
    sine_table = jnp.concatenate([jnp.sin(angles), jnp.sin(angles)], axis=-1)
    query_rotated = rotary_tables(
        queries.reshape(token_count, heads_dev, HEAD_WIDTH), cosine_table, sine_table
    ).astype(jnp.bfloat16)
    key_rotated = (
        rotary_tables(
            key_projected_rows.reshape(token_count, 1, HEAD_WIDTH), cosine_table, sine_table
        )
        .reshape(token_count, HEAD_WIDTH)
        .astype(jnp.bfloat16)
    )
    rotated_key_cache = lax.dynamic_slice_in_dim(
        jnp.where(valid_token_mask[:, None], key_rotated, zero_half_precision),
        offset,
        tile_width,
        1,
    )
    q_heads = query_rotated.reshape(GROUP_ROLLOUTS, ROLLOUT_SLOTS, heads_dev, HEAD_WIDTH)
    k_heads = key_rotated.reshape(GROUP_ROLLOUTS, ROLLOUT_SLOTS, HEAD_WIDTH)
    v_heads = value_rounded_rows.reshape(GROUP_ROLLOUTS, ROLLOUT_SLOTS, HEAD_WIDTH)
    scores = jnp.einsum(
        "rthd,rsd->rhts", q_heads, k_heads, preferred_element_type=jnp.float32
    ) / jnp.sqrt(jnp.float32(HEAD_WIDTH))
    causal = positions[None, :] <= positions[:, None]
    scores = jnp.where(causal, scores, -jnp.inf)
    row_max = jnp.max(scores, axis=-1, keepdims=True)
    weights = jnp.exp(scores - row_max)
    attn_probs = (weights / jnp.sum(weights, axis=-1, keepdims=True)).astype(jnp.bfloat16)
    context = jnp.einsum("rhts,rsd->rthd", attn_probs, v_heads, preferred_element_type=jnp.float32)
    context = jnp.where(valid_grid[:, :, None, None], context, 0.0).astype(jnp.bfloat16)
    context = context.reshape(token_count, heads_dev * HEAD_WIDTH)
    summed = lax.psum_scatter(
        lax.dot_general(
            w_out, context, (((0,), (1,)), ((), ())), preferred_element_type=jnp.float32
        ),
        "tp",
        scatter_dimension=0,
        tiled=True,
    )
    attended = summed.T
    layer_out = (hidden_in.astype(jnp.float32) + attended).astype(jnp.bfloat16)
    return (layer_out, rotated_key_cache, value_cache)


def solution(mesh):
    in_specs = (
        P("grp", "tp"),
        P("tp"),
        P("tp", None),
        P("tp"),
        P("tp", None),
        P(),
        P("tp", None),
        P(),
        P("tp", None),
        P("grp"),
    )
    out_specs = (P("grp", "tp"), P("grp", "tp"), P("grp", "tp"))
    return jax.shard_map(local, mesh=mesh, in_specs=in_specs, out_specs=out_specs, check_vma=False)
```

profile of v0, /device:TPU:0, one launch (start us, length us, event | category | flops | bytes accessed | tf_op | source)
XLA Modules:
  0.0 553.1 jit_solution(14490078671615261847)
XLA Ops:
  7.2 1.2 copy-done
  8.4 0.2 copy_bitcast_fusion
  8.6 1.7 broadcast_in_dim.63
  10.3 7.4 %all-to-all-start.1 = ((bf16[512,16,128]{2,0,1:T(8,128)(2,1)}), bf16[512,16,128]{2,0,1:T(8,128)(2,1)S(1)}, u32[]{:S(2)}, u32[]{:S(2)}) async-start(bf16[512,16,128]{2,0,1:T(8,128)(2,1)} %bitcast.7), calls=%async_computation.1 | async-start | bytes 4194304 | tf_op jit(solution)/shard_map/all_to_all | solution.py:71
  17.7 1.4 copy_bitcast_fusion.1
  19.1 39.7 %all-to-all-done.1 = bf16[512,16,128]{2,0,1:T(8,128)(2,1)S(1)} async-done(((bf16[512,16,128]{2,0,1:T(8,128)(2,1)}), bf16[512,16,128]{2,0,1:T(8,128)(2,1)S(1)}, u32[]{:S(2)}, u32[]{:S(2)}) %all-to-all-start.1) | async-done | bytes 2097184 | tf_op jit(solution)/shard_map/all_to_all | solution.py:71
  58.8 2.0 broadcast_in_dim.61
  60.8 11.2 %all-to-all-start = ((bf16[512,16,128]{2,0,1:T(8,128)(2,1)}), bf16[512,16,128]{2,0,1:T(8,128)(2,1)S(1)}, u32[]{:S(2)}, u32[]{:S(2)}) async-start(bf16[512,16,128]{2,0,1:T(8,128)(2,1)} %bitcast.1), calls=%async_computation | async-start | bytes 4194304 | tf_op jit(solution)/shard_map/all_to_all | solution.py:72
  72.0 11.6 %copy.71 = bf16[512,8192]{0,1:T(8,128)(2,1)} copy(bf16[512,8192]{1,0:T(8,128)(2,1)} %param.12) | data formatting | bytes 16777216 | tf_op args[2]
  83.6 29.5 %all-to-all-done = bf16[512,16,128]{2,0,1:T(8,128)(2,1)S(1)} async-done(((bf16[512,16,128]{2,0,1:T(8,128)(2,1)}), bf16[512,16,128]{2,0,1:T(8,128)(2,1)S(1)}, u32[]{:S(2)}, u32[]{:S(2)}) %all-to-all-start) | async-done | bytes 2097184 | tf_op jit(solution)/shard_map/all_to_all | solution.py:72
  113.1 11.4 %all-to-all-start.2 = ((bf16[512,16,512]{0,2,1:T(8,128)(2,1)}), bf16[512,16,512]{0,2,1:T(8,128)(2,1)}, u32[]{:S(2)}, u32[]{:S(2)}) async-start(bf16[512,16,512]{0,2,1:T(8,128)(2,1)} %bitcast.69), calls=%async_computation.2 | async-start | bytes 16777216 | tf_op jit(solution)/shard_map/all_to_all | solution.py:70
  124.5 0.0 all-gather.3.cloned.1.call-start
  124.6 0.7 all-gather.3.cloned.1.call-update
  125.3 0.0 reduce-scatter.2.cloned.1.call-start
  125.4 188.8 %all-gather = bf16[16,1,512]{2,1,0:T(2,128)(2,1)S(1)} all-gather(bf16[1,1,512]{2,1,0:T(2,128)(2,1)S(1)} %reshape.162), channel_id=1, replica_groups=mesh['grp'=2,'tp'=16] {'tp'}, dimensions={0}, use_global_device_ids=true | all-gather | bytes 17408 | tf_op jit(solution)/shard_map/all_gather | solution.py:44
  314.2 0.1 convert_element_type.107
  314.3 0.8 dynamic-slice_convert_fusion
  315.1 0.8 dynamic-slice_convert_fusion.1
  315.9 0.8 multiply_cosine_fusion
  316.6 0.8 pad_maximum_fusion
  317.5 0.1 iota_compare_fusion.1
  317.5 0.8 multiply_sine_fusion.1
  318.3 4.3 fusion.1
  322.6 0.3 copy-done.2
  322.9 3.6 convolution_add_fusion.1
  326.6 0.1 fusion.17
  326.7 0.2 fusion.19
  326.9 2.8 fusion.8
  329.8 12.5 %copy.72 = bf16[16,512,512]{2,1,0:T(8,128)(2,1)} copy(bf16[16,512,512]{1,2,0:T(8,128)(2,1)} %bitcast.17) | data formatting | bytes 16777216 | tf_op jit(solution)/shard_map/all_to_all | solution.py:70
  342.3 7.9 %convolution_add_fusion = f32[384,512]{1,0:T(8,128)S(1)} fusion(bf16[8192,512]{1,0:T(8,128)(2,1)} %bitcast.70, f32[512]{0:T(512)S(1)} %convert_element_type.111, bf16[384,8192]{1,0:T(8,128)(2,1)} %all-gather.3.cloned.1.call-done, f32[8192]{0:T(1024)S(1)} %bitcast.81, f32[384]{0:T(512)S(1)} %add_rsqrt_fusion), kind=kOutput, calls=%fused_computation.12 | convolution fusion | flops 3234004992 | bytes 15502848 | tf_op jit(solution)/shard_map/dot_general | solution.py:89
  350.1 0.3 copy.86
  350.4 0.3 reshape.159
  350.7 0.1 slice_negate_fusion
  350.8 0.4 concatenate.34
  351.1 0.3 copy.76
  351.4 0.4 concatenate.35
  351.8 0.3 copy.77
  352.1 2.6 bitcast_select_fusion
  354.7 1.7 fusion.30
  356.4 2.6 fusion.7
  359.0 0.3 copy.79
  359.3 9.7 %convolution_bitcast_fusion = f32[8192,384]{0,1:T(8,128)} fusion(bf16[512,8192]{1,0:T(8,128)(2,1)} %param.18, bf16[48,8,4,128]{3,2,1,0:T(4,128)(2,1)S(1)} %bitcast.71), kind=kOutput, calls=%fused_computation.6 | convolution fusion | flops 3221225472 | bytes 21364736 | tf_op jit(solution)/shard_map/dot_general | solution.py:130
  369.1 0.1 lt.59
  369.2 0.2 dynamic-slice_select_fusion
  369.4 0.7 copy.80
  370.1 0.7 copy.81
  370.8 173.5 %reduce-scatter.2.cloned.1.call-done = f32[512,384]{0,1:T(8,128)} async-done(((f32[8192,384]{0,1:T(8,128)}), f32[512,384]{0,1:T(8,128)}) %reduce-scatter.2.cloned.1.call-update) | async-done | bytes 786448 | tf_op jit(solution)/shard_map/reduce_scatter | solution.py:129
  544.3 2.0 fusion.11
  (28 shorter events, 0.2 us)
Async XLA Ops:
  7.2 1.2 copy-start
  10.3 48.5 %all-to-all-start.1 = ((bf16[512,16,128]{2,0,1:T(8,128)(2,1)}), bf16[512,16,128]{2,0,1:T(8,128)(2,1)S(1)}, u32[]{:S(2)}, u32[]{:S(2)}) async-start(bf16[512,16,128]{2,0,1:T(8,128)(2,1)} %bitcast.7), calls=%async_computation.1 | async-start | bytes 4194304 | tf_op jit(solution)/shard_map/all_to_all | solution.py:71
  58.8 2.0 copy-start.3
  60.8 52.3 %all-to-all-start = ((bf16[512,16,128]{2,0,1:T(8,128)(2,1)}), bf16[512,16,128]{2,0,1:T(8,128)(2,1)S(1)}, u32[]{:S(2)}, u32[]{:S(2)}) async-start(bf16[512,16,128]{2,0,1:T(8,128)(2,1)} %bitcast.1), calls=%async_computation | async-start | bytes 4194304 | tf_op jit(solution)/shard_map/all_to_all | solution.py:72
  113.1 12.2 %copy-start.7 = (bf16[512]{0:T(512)(128)(2,1)S(1)}, bf16[512]{0:T(512)(128)(2,1)}, u32[]{:S(2)}) copy-start(bf16[512]{0:T(512)(128)(2,1)} %param.11) | copy-start | bytes 3076
  113.1 201.2 %copy-start.8 = (bf16[512]{0:T(512)(128)(2,1)S(1)}, bf16[512]{0:T(512)(128)(2,1)}, u32[]{:S(2)}) copy-start(bf16[512]{0:T(512)(128)(2,1)} %param.13) | copy-start | bytes 3076
  113.1 204.3 %copy-start.9 = (s32[2]{0:T(128)S(1)}, s32[2]{0:T(128)}, u32[]{:S(2)}) copy-start(s32[2]{0:T(128)} %param.19) | copy-start | bytes 28
  113.1 216.6 %all-to-all-start.2 = ((bf16[512,16,512]{0,2,1:T(8,128)(2,1)}), bf16[512,16,512]{0,2,1:T(8,128)(2,1)}, u32[]{:S(2)}, u32[]{:S(2)}) async-start(bf16[512,16,512]{0,2,1:T(8,128)(2,1)} %bitcast.69), calls=%async_computation.2 | async-start | bytes 16777216 | tf_op jit(solution)/shard_map/all_to_all | solution.py:70
  124.5 193.8 %all-gather.3.cloned.1.call-start = ((), (), s32[]{:S(2)}) async-start(), calls=%async_computation.4 | async-start | bytes 6684672 | tf_op jit(solution)/shard_map/all_gather | solution.py:43
  125.3 419.0 %reduce-scatter.2.cloned.1.call-start = ((), (), s32[]{:S(2)}) async-start(), calls=%async_computation.5 | async-start | bytes 13369344 | tf_op jit(solution)/shard_map/reduce_scatter | solution.py:129
  314.2 12.4 %copy-start.5 = (f32[16,1,512]{2,1,0:T(1,128)}, f32[16,1,512]{2,1,0:T(1,128)S(1)}, u32[]{:S(2)}) copy-start(f32[16,1,512]{2,1,0:T(1,128)S(1)} %convert_element_type.117) | copy-start | bytes 98308
  318.3 4.6 copy-start.2
  329.8 12.5 %copy-start.6 = (f32[16,1,512]{2,1,0:T(1,128)S(1)}, f32[16,1,512]{2,1,0:T(1,128)}, u32[]{:S(2)}) copy-start(f32[16,1,512]{2,1,0:T(1,128)} %copy-done.5) | copy-start | bytes 98308
  369.1 177.2 %copy-start.1 = (bf16[512,1024]{1,0:T(8,128)(2,1)S(1)}, bf16[512,1024]{1,0:T(8,128)(2,1)}, u32[]{:S(2)}) copy-start(bf16[512,1024]{1,0:T(8,128)(2,1)} %param.14) | copy-start | bytes 3145732
  369.1 175.2 %copy-start.4 = (bf16[384,512]{1,0:T(8,128)(2,1)S(1)}, bf16[384,512]{1,0:T(8,128)(2,1)}, u32[]{:S(2)}) copy-start(bf16[384,512]{1,0:T(8,128)(2,1)} %param.10) | copy-start | bytes 1179652
Sparse Core Ops, SparseCore 0:
  127.5 188.0 all-gather.2
  369.2 175.0 reduce-scatter.1
where the time goes:
time: 554 us; the launch traced here: 553 us
  waiting for transfers between devices  243 us (44%)
  blocking collectives  189 us (34%)
  local copies, waits for them, and re-layouts  34.7 us (6%)
  matrix products  31 us (6%)
  starting transfers between devices  30.1 us (5%)
  between operations  14.3 us (3%)
  other arithmetic  10.8 us (2%)
    all_gather x1, blocking collectives, local(): lax.all_gather(norm_gain, 'tp', axis=0, tiled=True)  189 us
    reduce_scatter x1, waiting for transfers between devices, local(): lax.psum_scatter(lax.dot_general(w_out, context, (((0,), (1,)), ((), ()))...  173 us
    all_to_all x1, waiting for transfers between devices, local(): lax.all_to_all(key_repeated, 'tp', split_axis=1, concat_axis=0, tiled=True)  39.7 us
    all_to_all x1, waiting for transfers between devices, local(): lax.all_to_all(value_repeated, 'tp', split_axis=1, concat_axis=0, tiled=T...  29.5 us
    unnamed x24, local copies, waits for them, and re-layouts  14.6 us
    all_to_all x1, local copies, waits for them, and re-layouts, local(): lax.all_to_all(w_query, 'tp', split_axis=1, concat_axis=0, tiled=True)  12.5 us
    all_to_all x1, starting transfers between devices, local(): lax.all_to_all(w_query, 'tp', split_axis=1, concat_axis=0, tiled=True)  11.4 us
    all_to_all x1, starting transfers between devices, local(): lax.all_to_all(value_repeated, 'tp', split_axis=1, concat_axis=0, tiled=T...  11.2 us
  transfers between devices with their start and end apart: 5, of which 3 were waited for; matrix products, arithmetic and copies ran while one was open for 5% of the time, Pallas kernels for 0%

commit v1 on v0

--- a/solution.py
+++ b/solution.py
@@ -1,6 +1,9 @@
 import jax
 import jax.numpy as jnp
+import numpy as np
 from jax import lax
+from jax.experimental import pallas as pl
+from jax.experimental.pallas import tpu as pltpu
 from jax.sharding import PartitionSpec as P
 
 QUERY_HEADS = 64
@@ -12,6 +15,348 @@
 
 NORM_EPS = 1e-06
 ROPE_BASE = 1000000.0
+MODEL_WIDTH = 8192
+
+
+BF = jnp.bfloat16
+F32 = jnp.float32
+MESH = pl.DeviceIdType.MESH
+TOKENS = GROUP_ROLLOUTS * ROLLOUT_SLOTS
+PARTNERS = (1, 2, 3, 4, 8, 12)
+I16 = jnp.int16
+CODED = TOKENS + 16
+
+
+def flip(bit, mask):
+    return bit + mask - 2 * bit * mask
+
+
+def dotf(a, b):
+    return jnp.dot(a, b, preferred_element_type=F32)
+
+
+def code(ref, x):
+    top = jnp.maximum(jnp.max(jnp.abs(x), axis=0, keepdims=True), 1e-30)
+    exponent = jnp.ceil(jnp.log2(top))
+    ref[0:TOKENS, :] = jnp.round(x * (32000.0 * jnp.exp2(-exponent))).astype(jnp.int32).astype(I16)
+    ref[TOKENS:CODED, :] = jnp.broadcast_to(exponent, (16, x.shape[1])).astype(jnp.int32).astype(I16)
+
+
+def decode(ref, rows=slice(0, TOKENS), cols=slice(None)):
+    exponent = ref[TOKENS:CODED, cols].astype(jnp.int32).astype(F32)[0:1, :]
+    return ref[rows, cols].astype(jnp.int32).astype(F32) * (jnp.exp2(exponent) * (1.0 / 32000.0))
+
+
+def rotate(x, cos, sin_signed):
+    return x * cos + pltpu.roll(x, HEAD_WIDTH // 2, 1) * sin_signed
+
+
+def fused(
+    len_ref, x_ref, gain_ref, bq_ref, kb_ref, vb_ref, cos_ref, sin_ref, wq, wk, wv, wo,
+    out_ref, kc_ref, vc_ref,
+    xb, gb, nx, wqb, wkvb, wob,
+    r1, r1r, r2, r2r,
+    yas, yar, ybs, ybr, own, zas, zar, zbs, zbr,
+    kvbuf, ctxb, yos, yor, owno, zos, zor,
+    l_q, l_o, l_kv, c_send, c_recv,
+    wq_s, wq_r, wo_s, wo_r, r_s, r_r,
+    y_s, y_r, z_s, z_r,
+):
+    me = lax.axis_index("tp")
+    c = lax.rem(me, 2)
+    y = lax.rem(me // 2, 2)
+    zl = lax.rem(me // 4, 2)
+    zh = me // 8
+
+    def place(mask):
+        return 8 * flip(zh, mask // 8) + 4 * flip(zl, mask // 4 % 2) + 2 * flip(y, mask // 2 % 2) + flip(c, mask % 2)
+
+    def to(src, dst, ssem, rsem, mask):
+        return pltpu.make_async_remote_copy(
+            src_ref=src, dst_ref=dst, send_sem=ssem, recv_sem=rsem,
+            device_id={"tp": place(mask)}, device_id_type=MESH,
+        )
+
+    def z_mask(i):
+        return 3 - i
+
+    def column(i, my, mc):
+        return pl.ds(pl.multiple_of(place(4 * z_mask(i) + 2 * my + mc) * 512, 512), 512)
+
+    def load(w, buf, sem, i, h):
+        return pltpu.make_async_copy(w.at[:, column(i, 1 - h, 0)], buf.at[c, 2 * i + h], sem.at[2 * i + h])
+
+    def swap(w, buf, ss, rs, i, h):
+        return to(w.at[:, column(i, 1 - h, 1)], buf.at[c, 2 * i + h], ss.at[2 * i + h], rs.at[2 * i + h], 1)
+
+    barrier = pltpu.get_barrier_semaphore()
+    for mask in PARTNERS:
+        pl.semaphore_signal(barrier, inc=1, device_id={"tp": place(mask)}, device_id_type=MESH)
+
+    @pl.when(c == 0)
+    def _():
+        pltpu.make_async_copy(wk, wkvb.at[c], l_kv).start()
+
+    @pl.when(c == 1)
+    def _():
+        pltpu.make_async_copy(wv, wkvb.at[c], l_kv).start()
+
+    @pl.loop(0, 4)
+    def _(i):
+        load(wq, wqb, l_q, i, 0).start()
+        load(wq, wqb, l_q, i, 1).start()
+
+    xf = x_ref[...].astype(F32)
+    sq = xf * xf
+    sq = (sq[:, 0:128] + sq[:, 128:256]) + (sq[:, 256:384] + sq[:, 384:512])
+    r1[...] = jnp.broadcast_to(jnp.sum(sq.T, axis=0, keepdims=True), (8, TOKENS))
+    xb[pl.ds(c, 1)] = x_ref[...][None]
+    gb[pl.ds(c, 1)] = jnp.broadcast_to(gain_ref[...].astype(F32), (16, 512)).astype(BF)[None]
+
+    pl.semaphore_wait(barrier, len(PARTNERS))
+
+    for k in range(3):
+        to(r1, r1r.at[k], r_s.at[k], r_r.at[k], k + 1).start()
+    x_copy = to(x_ref, xb.at[c], c_send.at[0], c_recv.at[0], 1)
+    g_copy = to(gb.at[c], gb.at[c], c_send.at[1], c_recv.at[1], 1)
+    x_copy.start()
+    g_copy.start()
+    swap(wq, wqb, wq_s, wq_r, 0, 0).start()
+    swap(wq, wqb, wq_s, wq_r, 0, 1).start()
+
+    @pl.when(c == 0)
+    def _():
+        to(wv, wkvb.at[c], c_send.at[2], c_recv.at[2], 1).start()
+
+    @pl.when(c == 1)
+    def _():
+        to(wk, wkvb.at[c], c_send.at[2], c_recv.at[2], 1).start()
+
+    @pl.loop(1, 4)
+    def _(i):
+        swap(wq, wqb, wq_s, wq_r, i, 0).start()
+        swap(wq, wqb, wq_s, wq_r, i, 1).start()
+
+    for k in range(3):
+        to(r1, r1r.at[k], r_s.at[k], r_r.at[k], k + 1).wait()
+    r2[...] = (r1[...] + r1r[0]) + (r1r[1] + r1r[2])
+    for k in range(3):
+        to(r2, r2r.at[k], r_s.at[3 + k], r_r.at[3 + k], 4 * (k + 1)).start()
+    for k in range(3):
+        to(r2, r2r.at[k], r_s.at[3 + k], r_r.at[3 + k], 4 * (k + 1)).wait()
+    total = (r2[...] + r2r[0]) + (r2r[1] + r2r[2])
+    scale = lax.rsqrt(total[0:1, :] * (1.0 / MODEL_WIDTH) + NORM_EPS)
+    scale = jnp.broadcast_to(scale, (128, TOKENS)).T
+    x_copy.wait()
+    g_copy.wait()
+    for s in range(2):
+        for b in range(4):
+            cols = slice(128 * b, 128 * (b + 1))
+            nx[s, :, cols] = (
+                xb[s, :, cols].astype(F32) * scale * gb[s, 0:1, cols].astype(F32)
+            ).astype(BF)
+
+    @pl.loop(0, 4)
+    def _(i):
+        load(wo, wob, l_o, i, 0).start()
+        load(wo, wob, l_o, i, 1).start()
+        swap(wo, wob, wo_s, wo_r, i, 0).start()
+        swap(wo, wob, wo_s, wo_r, i, 1).start()
+
+    pltpu.make_async_copy(wk, wkvb.at[c], l_kv).wait()
+    to(wk, wkvb.at[c], c_send.at[2], c_recv.at[2], 1).wait()
+
+    def head(i, my):
+        return pl.ds(pl.multiple_of(place(4 * z_mask(i) + 2 * my) // 2 * 128, 128), 128)
+
+    def ya(i):
+        return to(yas.at[i], yar.at[i], y_s.at[i], y_r.at[i], 2)
+
+    def yb(i):
+        return to(ybs.at[i], ybr.at[i], y_s.at[4 + i], y_r.at[4 + i], 2)
+
+    def za(i):
+        return to(zas.at[i], zar.at[i], z_s.at[i], z_r.at[i], 4 * z_mask(i))
+
+    def zb(i):
+        return to(zbs.at[i], zbr.at[i], z_s.at[3 + i], z_r.at[3 + i], 4 * z_mask(i))
+
+    def yo(u):
+        return to(yos.at[u], yor.at[u], y_s.at[8 + u], y_r.at[8 + u], 2)
+
+    def zo(u):
+        return to(zos.at[u], zor.at[u], z_s.at[6 + u], z_r.at[6 + u], 4 * z_mask(u // 2))
+
+    left, right = slice(0, 256), slice(256, 512)
+
+    def project(act, w, j, cols):
+        return dotf(act[0], w[0, j, :, cols]) + dotf(act[1], w[1, j, :, cols])
+
+    def project_kv(i, my):
+        cols = head(i, my)
+        return dotf(nx[0], wkvb[0, :, cols]) + dotf(nx[1], wkvb[1, :, cols])
+
+    @pl.loop(0, 4)
+    def _(i):
+        load(wq, wqb, l_q, i, 0).wait()
+        swap(wq, wqb, wq_s, wq_r, i, 0).wait()
+        code(yas.at[i], project(nx, wqb, 2 * i, left))
+        ya(i).start()
+        code(ybs.at[i, :, 0:256], project(nx, wqb, 2 * i, right))
+        code(ybs.at[i, :, 256:384], project_kv(i, 1))
+        yb(i).start()
+
+    def own_part(i):
+        load(wq, wqb, l_q, i, 1).wait()
+        swap(wq, wqb, wq_s, wq_r, i, 1).wait()
+        own[:, left] = project(nx, wqb, 2 * i + 1, left)
+        own[:, right] = project(nx, wqb, 2 * i + 1, right)
+        own[:, 512:640] = project_kv(i, 0)
+
+    @pl.loop(0, 3)
+    def _(i):
+        own_part(i)
+        ya(i).wait()
+        code(zas.at[i], own[:, left] + decode(yar.at[i]))
+        za(i).start()
+        yb(i).wait()
+        code(zbs.at[i], own[:, 256:640] + decode(ybr.at[i]))
+        zb(i).start()
+
+    own_part(3)
+    ya(3).wait()
+    own[:, left] = own[:, left] + decode(yar.at[3])
+    yb(3).wait()
+    own[:, 256:640] = own[:, 256:640] + decode(ybr.at[3])
+    for i in range(3):
+        za(i).wait()
+        zb(i).wait()
+    kv = own[:, 512:640]
+    for i in range(3):
+        kv = kv + decode(zbr.at[i], cols=slice(256, 384))
+    at = pl.ds(pl.multiple_of(me // 2 * HEAD_WIDTH, HEAD_WIDTH), HEAD_WIDTH)
+    core = jnp.full((TOKENS, HEAD_WIDTH), c, jnp.int32)
+    kv = kv + jnp.where(core == 0, kb_ref[0:1, at].astype(F32), vb_ref[0:1, at].astype(F32))
+    cos, sin_signed = cos_ref[...], sin_ref[...]
+    kvbuf[pl.ds(c, 1)] = jnp.where(core == 0, rotate(kv, cos, sin_signed), kv).astype(BF)[None]
+    kv_copy = to(kvbuf.at[c], kvbuf.at[c], c_send.at[3], c_recv.at[3], 1)
+    kv_copy.start()
+
+    row = lax.broadcasted_iota(jnp.int32, (TOKENS, HEAD_WIDTH), 0)
+    ok = row < jnp.where(row < ROLLOUT_SLOTS, len_ref[0], len_ref[1] + ROLLOUT_SLOTS)
+    half = HEAD_WIDTH // 2
+
+    def cache(x):
+        x = jnp.where(ok, x.astype(F32), 0.0)
+        return jnp.where(core[:, :half] == 0, x[:, :half], x[:, half:]).astype(BF)
+
+    kv_copy.wait()
+    kc_ref[...] = cache(kvbuf[0])
+    vc_ref[...] = cache(kvbuf[1])
+
+    shape = (ROLLOUT_SLOTS, ROLLOUT_SLOTS)
+    causal = lax.broadcasted_iota(jnp.int32, shape, 1) <= lax.broadcasted_iota(jnp.int32, shape, 0)
+    for r in range(GROUP_ROLLOUTS):
+        rows = slice(ROLLOUT_SLOTS * r, ROLLOUT_SLOTS * (r + 1))
+        k, v = kvbuf[0, rows, :], kvbuf[1, rows, :]
+        for h in range(4):
+            cols = slice(128 * h, 128 * (h + 1))
+            zr, zcols = (zar, cols) if h < 2 else (zbr, slice(cols.start - 256, cols.stop - 256))
+            q = own[rows, cols] + decode(zr.at[0], rows, zcols)
+            q = q + (decode(zr.at[1], rows, zcols) + decode(zr.at[2], rows, zcols))
+            q = q + bq_ref[0:1, cols].astype(F32)
+            q = rotate(q, cos[rows], sin_signed[rows]).astype(BF)
+            s = lax.dot_general(q, k, (((1,), (1,)), ((), ())), preferred_element_type=F32)
+            s = jnp.where(causal, s / np.float32(np.sqrt(np.float32(HEAD_WIDTH))), -jnp.inf)
+            w = jnp.exp(s - jnp.max(s, axis=1, keepdims=True))
+            p = (w / jnp.sum(w, axis=1, keepdims=True)).astype(BF)
+            o = jnp.where(ok[rows], dotf(p, v), 0.0).astype(BF)
+            ctxb[pl.ds(c, 1), rows, cols] = o[None]
+    ctx_copy = to(ctxb.at[c], ctxb.at[c], c_send.at[4], c_recv.at[4], 1)
+    ctx_copy.start()
+    ctx_copy.wait()
+
+    @pl.loop(0, 4)
+    def _(i):
+        load(wo, wob, l_o, i, 0).wait()
+        swap(wo, wob, wo_s, wo_r, i, 0).wait()
+        code(yos.at[2 * i], project(ctxb, wob, 2 * i, left))
+        yo(2 * i).start()
+        code(yos.at[2 * i + 1], project(ctxb, wob, 2 * i, right))
+        yo(2 * i + 1).start()
+
+    def own_out(i):
+        load(wo, wob, l_o, i, 1).wait()
+        swap(wo, wob, wo_s, wo_r, i, 1).wait()
+        owno[:, left] = project(ctxb, wob, 2 * i + 1, left)
+        owno[:, right] = project(ctxb, wob, 2 * i + 1, right)
+
+    @pl.loop(0, 3)
+    def _(i):
+        own_out(i)
+        yo(2 * i).wait()
+        code(zos.at[2 * i], owno[:, left] + decode(yor.at[2 * i]))
+        zo(2 * i).start()
+        yo(2 * i + 1).wait()
+        code(zos.at[2 * i + 1], owno[:, right] + decode(yor.at[2 * i + 1]))
+        zo(2 * i + 1).start()
+
+    own_out(3)
+    for p, cols in enumerate((left, right)):
+        yo(6 + p).wait()
+        att = owno[:, cols] + decode(yor.at[6 + p])
+        for i in range(3):
+            zo(2 * i + p).wait()
+            att = att + decode(zor.at[2 * i + p])
+        out_ref[:, cols] = (x_ref[:, cols].astype(F32) + att).astype(BF)
+
+
+def local_fused(
+    hidden_in, norm_gain, w_query, b_query, key_weight_matrix, key_offset_bias,
+    value_weight_matrix, value_offset_bias, w_out, lengths,
+):
+    positions = np.tile(np.arange(ROLLOUT_SLOTS), GROUP_ROLLOUTS).astype(np.float64)
+    freq = ROPE_BASE ** (-2.0 * np.arange(HEAD_WIDTH // 2) / HEAD_WIDTH)
+    angles = positions[:, None] * freq[None, :]
+    cos = np.concatenate([np.cos(angles), np.cos(angles)], axis=1).astype(np.float32)
+    sin_signed = np.concatenate([-np.sin(angles), np.sin(angles)], axis=1).astype(np.float32)
+    vmem = pl.BlockSpec(memory_space=pltpu.VMEM)
+    hbm = pl.BlockSpec(memory_space=pl.ANY)
+    sem = pltpu.SemaphoreType.DMA
+    V = pltpu.VMEM
+    T = TOKENS
+    return pl.pallas_call(
+        fused,
+        out_shape=(
+            jax.ShapeDtypeStruct((T, 512), BF),
+            jax.ShapeDtypeStruct((T, HEAD_WIDTH // 2), BF),
+            jax.ShapeDtypeStruct((T, HEAD_WIDTH // 2), BF),
+        ),
+        in_specs=[pl.BlockSpec(memory_space=pltpu.SMEM)] + [vmem] * 7 + [hbm] * 4,
+        out_specs=(vmem, vmem, vmem),
+        scratch_shapes=[
+            V((2, T, 512), BF), V((2, 16, 512), BF), V((2, T, 512), BF),
+            V((2, 8, 512, 512), BF), V((2, 512, 1024), BF), V((2, 8, 512, 512), BF),
+            V((8, T), F32), V((3, 8, T), F32), V((8, T), F32), V((3, 8, T), F32),
+            V((4, CODED, 256), I16), V((4, CODED, 256), I16), V((4, CODED, 384), I16), V((4, CODED, 384), I16),
+            V((T, 640), F32),
+            V((3, CODED, 256), I16), V((3, CODED, 256), I16), V((3, CODED, 384), I16), V((3, CODED, 384), I16),
+            V((2, T, 128), BF), V((2, T, 512), BF),
+            V((8, CODED, 256), I16), V((8, CODED, 256), I16), V((T, 512), F32),
+            V((6, CODED, 256), I16), V((6, CODED, 256), I16),
+            sem((8,)), sem((8,)), sem, sem((5,)), sem((5,)),
+            sem((8,)), sem((8,)), sem((8,)), sem((8,)), sem((6,)), sem((6,)),
+            sem((16,)), sem((16,)), sem((12,)), sem((12,)),
+        ],
+        compiler_params=pltpu.CompilerParams(
+            collective_id=0, has_side_effects=True, vmem_limit_bytes=56 * 1024 * 1024
+        ),
+    )(
+        lengths, hidden_in, norm_gain[None, :], b_query[None, :],
+        key_offset_bias[None, :], value_offset_bias[None, :],
+        jnp.asarray(cos), jnp.asarray(sin_signed),
+        w_query, key_weight_matrix, value_weight_matrix, w_out,
+    )
 
 
 def rotary_tables(values, cosine_table, sine_table):
@@ -153,4 +498,5 @@
         P("grp"),
     )
     out_specs = (P("grp", "tp"), P("grp", "tp"), P("grp", "tp"))
-    return jax.shard_map(local, mesh=mesh, in_specs=in_specs, out_specs=out_specs, check_vma=False)
+    body = local_fused if mesh.shape["tp"] == 16 else local
+    return jax.shard_map(body, mesh=mesh, in_specs=in_specs, out_specs=out_specs, check_vma=False)

time: 554 us -> 128 us (0.23)
  waiting for transfers between devices: 243 us -> 0 us
  blocking collectives: 189 us -> 0 us
  Pallas kernels: 0 us -> 117 us
  matrix products: 31 us -> 0 us
  starting transfers between devices: 30.1 us -> 0 us
  local copies, waits for them, and re-layouts: 34.7 us -> 10 us
  between operations: 14.3 us -> 0.64 us
  other arithmetic: 10.8 us -> 0 us
    all_gather x1 -> x0, blocking collectives: 189 us -> none  [local(): lax.all_gather(norm_gain, 'tp', axis=0, tiled=True)]
    reduce_scatter x1 -> x0, waiting for transfers between devices: 173 us -> none  [local(): lax.psum_scatter(lax.dot_general(w_out, context, (((0,), (1,)), ((), ()))...]
    pallas_call x0 -> x1, Pallas kernels: none -> 117 us  [local_fused(): pl.pallas_call(fused, out_shape=(jax.ShapeDtypeStruct((T, 512), BF), jax....]
    all_to_all x3 -> x0, waiting for transfers between devices: 69.2 us -> none  [the longest x1 39.7 us: local(): lax.all_to_all(key_repeated, 'tp', split_axis=1, concat_axis=0, tiled=True)]
    all_to_all x3 -> x0, starting transfers between devices: 30 us -> none  [the longest x1 11.4 us: local(): lax.all_to_all(w_query, 'tp', split_axis=1, concat_axis=0, tiled=True)]
    dot_general x6 -> x0, matrix products: 29.3 us -> none  [the longest x1 9.74 us: local(): lax.dot_general(w_out, context, (((0,), (1,)), ((), ())), preferred_eleme...]
    unnamed x24 -> x1, local copies, waits for them, and re-layouts: 14.6 us -> 1.77 us
    all_to_all x1 -> x0, local copies, waits for them, and re-layouts: 12.5 us -> none  [local(): lax.all_to_all(w_query, 'tp', split_axis=1, concat_axis=0, tiled=True)]
  transfers between devices with their start and end apart: 5 -> 0, of which waited for: 3 -> 0; matrix products, arithmetic and copies ran while one was open for 5% -> 0% of each run, Pallas kernels for 0% -> 0%
where the time goes in v1:
time: 128 us; the launch traced here: 127 us
  Pallas kernels  117 us (91%)
  local copies, waits for them, and re-layouts  10 us (8%)
    pallas_call x1, Pallas kernels, local_fused(): pl.pallas_call(fused, out_shape=(jax.ShapeDtypeStruct((T, 512), BF), jax....  117 us
    pallas_call x2, local copies, waits for them, and re-layouts, local_fused(): pl.pallas_call(fused, out_shape=(jax.ShapeDtypeStruct((T, 512), BF), jax....  3.2 us

profile of v1, /device:TPU:0, one launch (start us, length us, event | category | flops | bytes accessed | tf_op | source)
XLA Modules:
  0.0 127.3 jit_solution(6334144068712374035)
XLA Ops:
  0.6 1.3 broadcast_in_dim.12.gain_ref
  1.9 1.3 broadcast_in_dim.13.bq_ref
  3.2 1.3 %broadcast_in_dim.14.kb_ref = bf16[1,1024]{1,0:T(2,128)(2,1)} reshape(bf16[1024]{0:T(1024)(128)(2,1)} %param.17) | data formatting | bytes 4096 | tf_op jit(solution)/shard_map/broadcast_in_dim | solution.py:356
  4.4 1.3 %broadcast_in_dim.15.vb_ref = bf16[1,1024]{1,0:T(2,128)(2,1)} reshape(bf16[1024]{0:T(1024)(128)(2,1)} %param.19) | data formatting | bytes 4096 | tf_op jit(solution)/shard_map/broadcast_in_dim | solution.py:356
  5.7 116.6 %shard_map.139 = (bf16[384,512]{1,0:T(8,128)(2,1)}, bf16[384,64]{1,0:T(8,128)(2,1)}, bf16[384,64]{1,0:T(8,128)(2,1)}) custom-call(s32[2]{0:T(128)} %len_ref.1, bf16[384,512]{1,0:T(8,128)(2,1)} %x_ref.1, bf16[1,512]{1,0:T(2,128)(2,1)} %broadcast_in_dim.12.gain_ref, bf16[1,512]{1,0:T(2,128)(2,1)} %broadcast_in_dim.13.bq_ref, ...), custom_call_target="tpu_custom_call" | custom-call | tf_op jit(solution)/shard_map/pallas_call | solution.py:328
  122.3 1.6 %copy.15 = bf16[384,64]{0,1:T(8,128)(2,1)} copy(bf16[384,64]{1,0:T(8,128)(2,1)} %get-tuple-element.4) | data formatting | bytes 98304 | tf_op jit(solution)/shard_map/pallas_call | solution.py:328
  123.9 1.6 %copy.16 = bf16[384,64]{0,1:T(8,128)(2,1)} copy(bf16[384,64]{1,0:T(8,128)(2,1)} %get-tuple-element.5) | data formatting | bytes 98304 | tf_op jit(solution)/shard_map/pallas_call | solution.py:328
  125.5 1.8 %copy.18 = bf16[384,512]{1,0:T(8,128)(2,1)} copy(bf16[384,512]{1,0:T(8,128)(2,1)} %get-tuple-element.9) | data formatting | bytes 786432

commit v2 on v1

--- a/solution.py
+++ b/solution.py
@@ -111,7 +111,7 @@
     sq = (sq[:, 0:128] + sq[:, 128:256]) + (sq[:, 256:384] + sq[:, 384:512])
     r1[...] = jnp.broadcast_to(jnp.sum(sq.T, axis=0, keepdims=True), (8, TOKENS))
     xb[pl.ds(c, 1)] = x_ref[...][None]
-    gb[pl.ds(c, 1)] = jnp.broadcast_to(gain_ref[...].astype(F32), (16, 512)).astype(BF)[None]
+    gb[pl.ds(c, 1)] = jnp.broadcast_to(gain_ref[...].astype(F32).reshape(1, 512), (16, 512)).astype(BF)[None]
 
     pl.semaphore_wait(barrier, len(PARTNERS))
 
@@ -234,9 +234,14 @@
     kv = own[:, 512:640]
     for i in range(3):
         kv = kv + decode(zbr.at[i], cols=slice(256, 384))
-    at = pl.ds(pl.multiple_of(me // 2 * HEAD_WIDTH, HEAD_WIDTH), HEAD_WIDTH)
+    kv_row = lax.broadcasted_iota(jnp.int32, (KEY_VALUE_HEADS, HEAD_WIDTH), 0)
     core = jnp.full((TOKENS, HEAD_WIDTH), c, jnp.int32)
-    kv = kv + jnp.where(core == 0, kb_ref[0:1, at].astype(F32), vb_ref[0:1, at].astype(F32))
+    bias = jnp.where(
+        core[0:KEY_VALUE_HEADS] == 0,
+        kb_ref[...].astype(F32).reshape(KEY_VALUE_HEADS, HEAD_WIDTH),
+        vb_ref[...].astype(F32).reshape(KEY_VALUE_HEADS, HEAD_WIDTH),
+    )
+    kv = kv + jnp.sum(jnp.where(kv_row == me // 2, bias, 0.0), axis=0, keepdims=True)
     cos, sin_signed = cos_ref[...], sin_ref[...]
     kvbuf[pl.ds(c, 1)] = jnp.where(core == 0, rotate(kv, cos, sin_signed), kv).astype(BF)[None]
     kv_copy = to(kvbuf.at[c], kvbuf.at[c], c_send.at[3], c_recv.at[3], 1)
@@ -248,7 +253,7 @@
 
     def cache(x):
         x = jnp.where(ok, x.astype(F32), 0.0)
-        return jnp.where(core[:, :half] == 0, x[:, :half], x[:, half:]).astype(BF)
+        return jnp.where(core[:, :half] == 0, x[:, :half], x[:, half:]).T.astype(BF)
 
     kv_copy.wait()
     kc_ref[...] = cache(kvbuf[0])
@@ -256,6 +261,7 @@
 
     shape = (ROLLOUT_SLOTS, ROLLOUT_SLOTS)
     causal = lax.broadcasted_iota(jnp.int32, shape, 1) <= lax.broadcasted_iota(jnp.int32, shape, 0)
+    bq = bq_ref[...].astype(F32).reshape(1, 512)
     for r in range(GROUP_ROLLOUTS):
         rows = slice(ROLLOUT_SLOTS * r, ROLLOUT_SLOTS * (r + 1))
         k, v = kvbuf[0, rows, :], kvbuf[1, rows, :]
@@ -264,7 +270,7 @@
             zr, zcols = (zar, cols) if h < 2 else (zbr, slice(cols.start - 256, cols.stop - 256))
             q = own[rows, cols] + decode(zr.at[0], rows, zcols)
             q = q + (decode(zr.at[1], rows, zcols) + decode(zr.at[2], rows, zcols))
-            q = q + bq_ref[0:1, cols].astype(F32)
+            q = q + bq[:, cols]
             q = rotate(q, cos[rows], sin_signed[rows]).astype(BF)
             s = lax.dot_general(q, k, (((1,), (1,)), ((), ())), preferred_element_type=F32)
             s = jnp.where(causal, s / np.float32(np.sqrt(np.float32(HEAD_WIDTH))), -jnp.inf)
@@ -325,12 +331,12 @@
     sem = pltpu.SemaphoreType.DMA
     V = pltpu.VMEM
     T = TOKENS
-    return pl.pallas_call(
+    out, kc, vc = pl.pallas_call(
         fused,
         out_shape=(
             jax.ShapeDtypeStruct((T, 512), BF),
-            jax.ShapeDtypeStruct((T, HEAD_WIDTH // 2), BF),
-            jax.ShapeDtypeStruct((T, HEAD_WIDTH // 2), BF),
+            jax.ShapeDtypeStruct((HEAD_WIDTH // 2, T), BF),
+            jax.ShapeDtypeStruct((HEAD_WIDTH // 2, T), BF),
         ),
         in_specs=[pl.BlockSpec(memory_space=pltpu.SMEM)] + [vmem] * 7 + [hbm] * 4,
         out_specs=(vmem, vmem, vmem),
@@ -352,11 +358,11 @@
             collective_id=0, has_side_effects=True, vmem_limit_bytes=56 * 1024 * 1024
         ),
     )(
-        lengths, hidden_in, norm_gain[None, :], b_query[None, :],
-        key_offset_bias[None, :], value_offset_bias[None, :],
+        lengths, hidden_in, norm_gain, b_query, key_offset_bias, value_offset_bias,
         jnp.asarray(cos), jnp.asarray(sin_signed),
         w_query, key_weight_matrix, value_weight_matrix, w_out,
     )
+    return out, kc.T, vc.T
 
 
 def rotary_tables(values, cosine_table, sine_table):

time: 128 us -> 122 us (0.953)
  local copies, waits for them, and re-layouts: 10 us -> 4.61 us
    broadcast_in_dim x4 -> x0, local copies, waits for them, and re-layouts: 5.08 us -> none  [the longest x1 1.28 us: local_fused(): key_offset_bias[None, :]]
    pallas_call x2 -> x0, local copies, waits for them, and re-layouts: 3.2 us -> none  [local_fused(): pl.pallas_call(fused, out_shape=(jax.ShapeDtypeStruct((T, 512), BF), jax....]
    unnamed x1 -> x3, local copies, waits for them, and re-layouts: 1.77 us -> 4.61 us
where the time goes in v2:
time: 122 us
  Pallas kernels  117 us (96%)
  local copies, waits for them, and re-layouts  4.61 us (4%)
    pallas_call x1, Pallas kernels, local_fused(): pl.pallas_call(fused, out_shape=(jax.ShapeDtypeStruct((T, 512), BF), jax....  117 us
    unnamed x3, local copies, waits for them, and re-layouts  4.61 us

profile of v2, /device:TPU:0, one launch (start us, length us, event | category | flops | bytes accessed | tf_op | source)
XLA Modules:
  0.0 122.0 jit_solution(2986515103910324457)
XLA Ops:
  0.6 116.7 %shard_map.139 = (bf16[384,512]{1,0:T(8,128)(2,1)}, bf16[64,384]{1,0:T(8,128)(2,1)}, bf16[64,384]{1,0:T(8,128)(2,1)}) custom-call(s32[2]{0:T(128)} %len_ref.1, bf16[384,512]{1,0:T(8,128)(2,1)} %x_ref.1, bf16[512]{0:T(512)(128)(2,1)} %gain_ref.1, bf16[512]{0:T(512)(128)(2,1)} %bq_ref.1, bf16[1024]{0:T(1024)(128)(2,1)} %kb_ref.1, bf16[1024]{0:T(1024)(128)(2,1)} %vb_ref.1, ...), custom_call_target="tpu_custom_call" | custom-call | tf_op jit(solution)/shard_map/pallas_call | solution.py:334
  117.4 1.8 %copy.18 = bf16[384,512]{1,0:T(8,128)(2,1)} copy(bf16[384,512]{1,0:T(8,128)(2,1)} %get-tuple-element.12) | data formatting | bytes 786432
  119.1 1.4 %copy.19 = bf16[384,64]{0,1:T(8,128)(2,1)} copy(bf16[384,64]{0,1:T(8,128)(2,1)} %bitcast.3) | data formatting | bytes 98304
  120.5 1.4 %copy.20 = bf16[384,64]{0,1:T(8,128)(2,1)} copy(bf16[384,64]{0,1:T(8,128)(2,1)} %bitcast.2) | data formatting | bytes 98304
